TPU v7x, 512 devices: a whole 4x8x8 slice. The times are simulated.
512 devices in a mesh: pts: 64 (over x, z, core), ctr: 8 (over y).
Axes of the slice: x: 4, y: 8, z: 8, core: 2. Of those that a mesh axis runs over, the one named last changes fastest.
Arguments:
- points: bfloat16 [65536, 512], P('pts'), may hold values from -16 to 16
- centres: bfloat16 [16384, 512], P('ctr'), may hold values from -16 to 16
- vector: float32 [32, 16384], P(None, 'ctr'), may hold values from -6144 to 6144
- factor: float32 [16384, 16384], P('pts', 'ctr'), may hold values from -1 to 1, as said below
Outputs:
- update: float32 [32, 16384], P(None, 'ctr')
Inputs may be any that keep to these rules, and one draw needn't show every extreme that they name: `factor`: entries below the diagonal blocks of 4096 by 4096 are zero.
All inputs are finite; a program needn't handle non-finite values.
Results may differ from a plain program's by a relative error of at most 0.0029.
Values sent between devices are 32-bit elements; how exact they have to be, the bound alone decides.
A program may use at most 64 MiB of HBM per device.

v0:
```python
import jax
import jax.numpy as jnp
from jax import lax
from jax.sharding import PartitionSpec as P

NBLK = 4


def broadcast(x, axis, root):
    mine = lax.axis_index(axis) == root
    return lax.psum(jnp.where(mine, x, jnp.zeros_like(x)), axis)


def kernel_tile(point_rows, centre_rows):
    inner_prods = lax.dot_general(
        point_rows, centre_rows, (((1,), (1,)), ((), ())), preferred_element_type=jnp.float32
    )
    point_norms = jnp.sum(jnp.square(point_rows.astype(jnp.float32)), axis=1)
    centre_norms = jnp.sum(jnp.square(centre_rows.astype(jnp.float32)), axis=1)
    distance = point_norms[:, None] + centre_norms[None, :] - 2.0 * inner_prods
    return jnp.exp(-(8.0 / point_rows.shape[1]) * distance).astype(jnp.bfloat16)


def body(points, centres, vector, factor):
    point_count = points.shape[0] * lax.axis_size("pts")
    centre_rows = centres.shape[0]
    block_size = centre_rows * lax.axis_size("ctr") // NBLK
    row_count = factor.shape[0]
    fold_ratio = lax.axis_size("pts") // lax.axis_size("ctr")
    point_group = lax.axis_index("pts")
    centre_group = lax.axis_index("ctr")
    kernel = kernel_tile(points, centres)
    images = lax.psum(
        lax.dot_general(
            vector.astype(jnp.bfloat16),
            kernel,
            (((1,), (1,)), ((), ())),
            preferred_element_type=jnp.float32,
        ),
        "ctr",
    )
    images = lax.optimization_barrier(images)
    images_low = (images / point_count).astype(jnp.bfloat16)
    partial_sum = jnp.dot(images_low, kernel, preferred_element_type=jnp.float32)
    col_block = (
        centre_group * centre_rows + jnp.arange(centre_rows, dtype=jnp.int32)
    ) // block_size
    row_block = (point_group * row_count + jnp.arange(row_count, dtype=jnp.int32)) // block_size
    slice_start = point_group % fold_ratio * row_count
    source_group = point_group // fold_ratio

    def to_rows(columns):
        slice_piece = lax.dynamic_slice_in_dim(columns, slice_start, row_count, 1)
        return broadcast(slice_piece, "ctr", source_group)

    def spread(row_values):
        return jnp.dot(
            row_values, factor, precision=lax.Precision.HIGHEST, preferred_element_type=jnp.float32
        )

    update = jnp.zeros((vector.shape[0], centre_rows), jnp.float32)
    update_rows = jnp.zeros((vector.shape[0], row_count), jnp.float32)
    kernel_sum = lax.psum(partial_sum, "pts")
    for block_idx in range(NBLK):
        if block_idx == 0:
            residual = kernel_sum
        else:
            residual = kernel_sum - lax.psum(spread(update_rows), "pts")
        rows_part = jnp.where((row_block == block_idx)[None, :], to_rows(residual), 0.0)
        solved = lax.psum(spread(rows_part), "pts")
        update = update + jnp.where((col_block == block_idx)[None, :], solved, 0.0)
        if block_idx + 1 < NBLK:
            update_rows = to_rows(update)
    return update


def solution(mesh):
    placed = (P("pts", None), P("ctr", None), P(None, "ctr"), P("pts", "ctr"))
    return jax.shard_map(
        body, mesh=mesh, in_specs=placed, out_specs=P(None, "ctr"), check_vma=False
    )
```

profile of v0, /device:TPU:57, one launch (start us, length us, event | category | flops | bytes accessed | tf_op | source)
XLA Modules:
  0.0 1797.1 jit_solution(1586242467137420171)
XLA Ops:
  6.5 2.2 multiply_reduce_fusion
  8.8 0.3 multiply_reduce_fusion.1
  9.1 0.2 copy-done.2
  9.2 2.9 exponential_convert_fusion
  12.2 1.9 copy-done.1
  14.1 2.1 convolution_bitcast_fusion
  16.2 0.0 all-reduce.12.cloned.1.call-start
  16.2 77.5 %all-reduce.10.cloned.1.call-done = f32[32,1024]{0,1:T(8,128)} async-done(((f32[32,1024]{0,1:T(8,128)}), f32[32,1024]{0,1:T(8,128)}) %all-reduce.10.cloned.1.call-update) | async-done | bytes 131088 | tf_op jit(solution)/shard_map/psum | solution.py:33
  93.7 3.9 fusion
  97.6 0.0 all-reduce.12.cloned.1.call-update
  97.6 0.0 all-reduce.14.cloned.1.call-start
  97.7 191.1 %all-reduce.12.cloned.1.call-done = f32[32,2048]{1,0:T(8,128)} async-done(((f32[32,2048]{1,0:T(8,128)}), f32[32,2048]{1,0:T(8,128)}) %all-reduce.12.cloned.1.call-update) | async-done | bytes 262160 | tf_op jit(solution)/shard_map/psum | solution.py:63
  288.8 0.8 dynamic-slice_select_fusion.3
  289.6 20.1 %psum.114 = f32[32,256]{1,0:T(8,128)S(1)} all-reduce(f32[32,256]{1,0:T(8,128)S(1)} %dynamic-slice_select_fusion.3), channel_id=1, replica_groups=mesh['pts'=64,'ctr'=8] {'ctr'}, use_global_device_ids=true, to_apply=%region_4.5 | all-reduce | flops 8192 | bytes 65536 | tf_op jit(solution)/shard_map/psum | solution.py:11
  309.7 2.0 fusion.12
  311.7 0.0 all-reduce.14.cloned.1.call-update
  311.7 0.0 all-reduce.16.cloned.1.call-start
  311.8 191.2 %all-reduce.14.cloned.1.call-done = f32[32,2048]{1,0:T(8,128)} async-done(((f32[32,2048]{1,0:T(8,128)}), f32[32,2048]{1,0:T(8,128)}) %all-reduce.14.cloned.1.call-update) | async-done | bytes 262160 | tf_op jit(solution)/shard_map/psum | solution.py:70
  503.0 1.0 broadcast_select_fusion
  504.0 20.1 %psum.116 = f32[32,256]{1,0:T(8,128)S(1)} all-reduce(f32[32,256]{1,0:T(8,128)S(1)} %dynamic-slice_select_fusion.2), channel_id=1, replica_groups=mesh['pts'=64,'ctr'=8] {'ctr'}, use_global_device_ids=true, to_apply=%region_6.7 | all-reduce | flops 8192 | bytes 65536 | tf_op jit(solution)/shard_map/psum | solution.py:11
  524.2 2.0 fusion.30
  526.2 0.0 all-reduce.18.cloned.1.call-start
  526.3 191.2 %all-reduce.16.cloned.1.call-done = f32[32,2048]{1,0:T(8,128)} async-done(((f32[32,2048]{1,0:T(8,128)}), f32[32,2048]{1,0:T(8,128)}) %all-reduce.16.cloned.1.call-update) | async-done | bytes 262160 | tf_op jit(solution)/shard_map/psum | solution.py:68
  717.5 0.8 fusion.5
  718.2 20.1 %psum.118 = f32[32,256]{1,0:T(8,128)S(1)} all-reduce(f32[32,256]{1,0:T(8,128)S(1)} %fusion.5), channel_id=1, replica_groups=mesh['pts'=64,'ctr'=8] {'ctr'}, use_global_device_ids=true, to_apply=%region_8.9 | all-reduce | flops 8192 | bytes 65536 | tf_op jit(solution)/shard_map/psum | solution.py:11
  738.4 2.0 fusion.10
  740.4 0.0 all-reduce.20.cloned.1.call-start
  740.5 191.2 %all-reduce.18.cloned.1.call-done = f32[32,2048]{1,0:T(8,128)} async-done(((f32[32,2048]{1,0:T(8,128)}), f32[32,2048]{1,0:T(8,128)}) %all-reduce.18.cloned.1.call-update) | async-done | bytes 262160 | tf_op jit(solution)/shard_map/psum | solution.py:70
  931.6 1.0 select_add_fusion.2
  932.6 20.1 %psum.120 = f32[32,256]{1,0:T(8,128)S(1)} all-reduce(f32[32,256]{1,0:T(8,128)S(1)} %dynamic-slice_select_fusion.1), channel_id=1, replica_groups=mesh['pts'=64,'ctr'=8] {'ctr'}, use_global_device_ids=true, to_apply=%region_10.11 | all-reduce | flops 8192 | bytes 65536 | tf_op jit(solution)/shard_map/psum | solution.py:11
  952.8 2.0 fusion.31
  954.8 0.0 all-reduce.22.cloned.1.call-start
  954.9 191.2 %all-reduce.20.cloned.1.call-done = f32[32,2048]{1,0:T(8,128)} async-done(((f32[32,2048]{1,0:T(8,128)}), f32[32,2048]{1,0:T(8,128)}) %all-reduce.20.cloned.1.call-update) | async-done | bytes 262160 | tf_op jit(solution)/shard_map/psum | solution.py:68
  1146.1 0.8 fusion.4
  1146.9 20.1 %psum.122 = f32[32,256]{1,0:T(8,128)S(1)} all-reduce(f32[32,256]{1,0:T(8,128)S(1)} %fusion.4), channel_id=1, replica_groups=mesh['pts'=64,'ctr'=8] {'ctr'}, use_global_device_ids=true, to_apply=%region_12.13 | all-reduce | flops 8192 | bytes 65536 | tf_op jit(solution)/shard_map/psum | solution.py:11
  1167.0 2.0 fusion.8
  1169.0 0.0 all-reduce.24.cloned.1.call-start
  1169.1 191.2 %all-reduce.22.cloned.1.call-done = f32[32,2048]{1,0:T(8,128)} async-done(((f32[32,2048]{1,0:T(8,128)}), f32[32,2048]{1,0:T(8,128)}) %all-reduce.22.cloned.1.call-update) | async-done | bytes 262160 | tf_op jit(solution)/shard_map/psum | solution.py:70
  1360.2 1.0 select_add_fusion.1
  1361.2 20.2 %psum.124 = f32[32,256]{1,0:T(8,128)S(1)} all-reduce(f32[32,256]{1,0:T(8,128)S(1)} %dynamic-slice_select_fusion), channel_id=1, replica_groups=mesh['pts'=64,'ctr'=8] {'ctr'}, use_global_device_ids=true, to_apply=%region_14.15 | all-reduce | flops 8192 | bytes 65536 | tf_op jit(solution)/shard_map/psum | solution.py:11
  1381.4 2.0 fusion.32
  1383.4 0.0 all-reduce.26.cloned.1.call-start
  1383.5 191.2 %all-reduce.24.cloned.1.call-done = f32[32,2048]{1,0:T(8,128)} async-done(((f32[32,2048]{1,0:T(8,128)}), f32[32,2048]{1,0:T(8,128)}) %all-reduce.24.cloned.1.call-update) | async-done | bytes 262160 | tf_op jit(solution)/shard_map/psum | solution.py:68
  1574.7 0.8 fusion.3
  1575.5 20.1 %psum.126 = f32[32,256]{1,0:T(8,128)S(1)} all-reduce(f32[32,256]{1,0:T(8,128)S(1)} %fusion.3), channel_id=1, replica_groups=mesh['pts'=64,'ctr'=8] {'ctr'}, use_global_device_ids=true, to_apply=%region_16.17 | all-reduce | flops 8192 | bytes 65536 | tf_op jit(solution)/shard_map/psum | solution.py:11
  1595.6 2.0 fusion.6
  1597.7 191.2 %all-reduce.26.cloned.1.call-done = f32[32,2048]{1,0:T(8,128)} async-done(((f32[32,2048]{1,0:T(8,128)}), f32[32,2048]{1,0:T(8,128)}) %all-reduce.26.cloned.1.call-update) | async-done | bytes 262160 | tf_op jit(solution)/shard_map/psum | solution.py:70
  1788.8 1.7 select_add_fusion
  (29 shorter events, 0.3 us)
Async XLA Ops:
  6.5 303.2 %copy-start = (f32[256,2048]{1,0:T(8,128)S(1)}, f32[256,2048]{1,0:T(8,128)}, u32[]{:S(2)}) copy-start(f32[256,2048]{1,0:T(8,128)} %param.7) | copy-start | bytes 6291460
  6.5 2.2 copy-start.4
  6.5 87.2 %all-reduce.10.cloned.1.call-start = ((), (), s32[]{:S(2)}) async-start(), calls=%async_computation | async-start | bytes 1048576 | tf_op jit(solution)/shard_map/psum | solution.py:33
  6.5 2.7 copy-start.2
  9.2 4.9 copy-start.5
  12.2 1.9 copy-start.1
  16.2 272.6 %all-reduce.12.cloned.1.call-start = ((), (), s32[]{:S(2)}) async-start(), calls=%async_computation.1 | async-start | bytes 524288 | tf_op jit(solution)/shard_map/psum | solution.py:63
  97.6 405.4 %all-reduce.14.cloned.1.call-start = ((), (), s32[]{:S(2)}) async-start(), calls=%async_computation.2 | async-start | bytes 524288 | tf_op jit(solution)/shard_map/psum | solution.py:70
  311.7 405.7 %all-reduce.16.cloned.1.call-start = ((), (), s32[]{:S(2)}) async-start(), calls=%async_computation.3 | async-start | bytes 524288 | tf_op jit(solution)/shard_map/psum | solution.py:68
  526.2 405.5 %copy-start.3 = (f32[32,2048]{1,0:T(8,128)S(1)}, f32[32,2048]{1,0:T(8,128)}, u32[]{:S(2)}) copy-start(f32[32,2048]{1,0:T(8,128)} %all-reduce.14.cloned.1.call-done) | copy-start | bytes 786436
  526.2 405.4 %all-reduce.18.cloned.1.call-start = ((), (), s32[]{:S(2)}) async-start(), calls=%async_computation.4 | async-start | bytes 524288 | tf_op jit(solution)/shard_map/psum | solution.py:70
  740.4 405.7 %all-reduce.20.cloned.1.call-start = ((), (), s32[]{:S(2)}) async-start(), calls=%async_computation.5 | async-start | bytes 524288 | tf_op jit(solution)/shard_map/psum | solution.py:68
  954.8 405.4 %all-reduce.22.cloned.1.call-start = ((), (), s32[]{:S(2)}) async-start(), calls=%async_computation.6 | async-start | bytes 524288 | tf_op jit(solution)/shard_map/psum | solution.py:70
  1169.0 405.7 %all-reduce.24.cloned.1.call-start = ((), (), s32[]{:S(2)}) async-start(), calls=%async_computation.7 | async-start | bytes 524288 | tf_op jit(solution)/shard_map/psum | solution.py:68
  1383.4 405.4 %all-reduce.26.cloned.1.call-start = ((), (), s32[]{:S(2)}) async-start(), calls=%async_computation.8 | async-start | bytes 524288 | tf_op jit(solution)/shard_map/psum | solution.py:70
Sparse Core Ops, SparseCore 0:
  16.3 77.3 all-reduce.9
  97.8 191.0 all-reduce.11
  311.9 191.1 all-reduce.13
  526.3 191.0 all-reduce.15
  740.5 191.0 all-reduce.17
  954.9 191.0 all-reduce.19
  1169.1 191.0 all-reduce.21
  1383.6 191.1 all-reduce.23
  1597.8 191.0 all-reduce.25
where the time goes:
time: 1800 us
  waiting for transfers between devices  1610 us (89%)
  blocking collectives  141 us (8%)
  matrix products  22.9 us (1%)
    psum x4, waiting for transfers between devices, body(): solved = lax.psum(spread(rows_part), 'pts')  765 us
    psum x3, waiting for transfers between devices, body(): residual = kernel_sum - lax.psum(spread(update_rows), 'pts')  574 us
    psum x1, waiting for transfers between devices, body(): kernel_sum = lax.psum(partial_sum, 'pts')  191 us
    psum x7, blocking collectives, broadcast(): return lax.psum(jnp.where(mine, x, jnp.zeros_like(x)), axis)  141 us
    psum x1, waiting for transfers between devices, body(): lax.psum(lax.dot_general(vector.astype(jnp.bfloat16), kernel, (((1,), (1,...  77.5 us
  transfers between devices with their start and end apart: 9, of which 9 were waited for; matrix products, arithmetic and copies ran while one was open for 0% of the time, Pallas kernels for 0%

commit v1 on v0

v1 whole, which is shorter than its diff:
```python
import jax
import jax.numpy as jnp
from jax import lax
from jax.experimental import pallas as pl
from jax.experimental.pallas import tpu as pltpu
from jax.sharding import PartitionSpec as P

F32, BF16 = jnp.float32, jnp.bfloat16
MESH = pl.DeviceIdType.MESH
NN = (((1,), (0,)), ((), ()))
NT = (((1,), (1,)), ((), ()))
PT = 256
S_IR, S_IG, S_TC, S_FX, S_RT, S_X, S_G, S_RA, S_B, S_O1, S_O2, S_END = (
    0, 8, 16, 17, 18, 26, 27, 31, 39, 51, 55, 71)
(R_IR, R_IG, R_TC, R_FX, R_RT, R_X, R_IN, R_AB, R_O1, R_O2, L_C, L_P, L_V, R_END) = (
    0, 1, 2, 3, 4, 5, 6, 7, 11, 12, 13, 14, 15, 16)


def device(x, y, z, c):
    return ((x * 8 + z) * 2 + c, y)


def sweep_kernel(
    points, centres, vector, factor, out,
    pts, cen, vec, norm_row, kmat, fraw, fhigh, flow,
    im_src, im_rs, ag_src, im_ag, im_low, t_src, t_rc, rs_src, rs_t, x_src, x_buf,
    s_src, inp, ab_src, rs_ab, u_src, o_buf, ssem, rsem,
):
    p, y = lax.axis_index("pts"), lax.axis_index("ctr")
    x, z, c = p // 16, (p // 2) % 8, p % 2
    k, h = y // 2, y % 2
    diag, works, below = x == k, x <= k, x < k

    def send(src, dst, s, r, dev, own=None):
        def remote():
            pltpu.make_async_remote_copy(
                src_ref=src, dst_ref=dst, send_sem=ssem.at[s], recv_sem=rsem.at[r],
                device_id=dev, device_id_type=MESH).start()
        if own is None:
            remote()
        else:
            pl.when(jnp.logical_not(own))(remote)

            @pl.when(own)
            def _():
                pltpu.make_async_copy(src, dst, rsem.at[r]).start()

    def sent(src, s, dev, own=None):
        def finish():
            pltpu.make_async_remote_copy(
                src_ref=src, dst_ref=src, send_sem=ssem.at[s], recv_sem=rsem.at[0],
                device_id=dev, device_id_type=MESH).wait_send()
        if own is None:
            finish()
        else:
            pl.when(jnp.logical_not(own))(finish)

    def arrived(buf, r):
        pltpu.make_async_copy(buf, buf, rsem.at[r]).wait()

    def each(n, f):
        def step(i, carry):
            f(i)
            return carry
        lax.fori_loop(0, n, step, 0)

    load_c = pltpu.make_async_copy(centres, cen, rsem.at[L_C])
    load_p = pltpu.make_async_copy(points, pts, rsem.at[L_P])
    load_v = pltpu.make_async_copy(vector, vec, rsem.at[L_V])
    load_c.start()
    load_p.start()
    load_v.start()

    barrier = pltpu.get_barrier_semaphore()

    def greet(dev):
        pl.semaphore_signal(barrier, inc=1, device_id=dev, device_id_type=MESH)

    each(7, lambda i: greet(device(x, (y + 1 + i) % 8, z, c)))
    each(3, lambda i: greet(device(x, 2 * k + (h + (i + 1) // 2) % 2, z, (c + (i + 1) % 2) % 2)))
    rs_own = z // 2 == 2 * h + c
    rs_y, rs_c = 2 * k + z // 4, (z // 2) % 2

    def greet_rs(i):
        @pl.when(jnp.logical_not(rs_own & (i == z)))
        def _():
            greet(device(x, rs_y, i, rs_c))
    each(8, greet_rs)

    def greet_out(i):
        dev = (2 * k + i // 2 % 2, 4 * h + i // 4, i % 2)

        @pl.when(jnp.logical_not((dev[0] == y) & (dev[1] == z) & (dev[2] == c)))
        def _():
            greet(device(x, *dev))
    each(16, greet_out)
    out_own = z // 4 == h

    @pl.when(diag)
    def _():
        each(3, lambda i: greet(device((x + 1 + i) % 4, y, z, c)))
        each(8 * k, lambda i: greet(device(i // 8, rs_y, i % 8, rs_c)))

    @pl.when(jnp.logical_not(diag))
    def _():
        greet(device(k, y, z, c))

    @pl.when(below)
    def _():
        each(4, lambda i: greet(device(x, 2 * x + i // 2, z, i % 2)))

    load_c.wait()
    squares = jnp.square(cen[...].astype(F32))
    folded = (squares[:, 0:128] + squares[:, 128:256]) + (squares[:, 256:384] + squares[:, 384:512])
    norm_row[...] = jnp.sum(folded.T, axis=0, keepdims=True) * (1.0 / 64.0)
    load_p.wait()
    load_v.wait()

    def kernel_step(i):
        rows = pl.ds(pl.multiple_of(i * PT, PT), PT)
        pt = pts[rows, :]
        prods = lax.dot_general(pt, cen[...], NT, preferred_element_type=F32)
        norms = jnp.sum(jnp.square(pt.astype(F32)), axis=1, keepdims=True) * (1.0 / 64.0)
        kern = jnp.exp(prods * (1.0 / 32.0) - (norms + norm_row[...])).astype(BF16)
        kmat[rows, :] = kern
        images = lax.dot_general(vec[...].astype(BF16), kern, NT, preferred_element_type=F32)
        im_src[2 * i] = images[:, 0:128]
        im_src[2 * i + 1] = images[:, 128:256]
    each(4, kernel_step)

    own_count = jnp.where(rs_own, 1, 0) + jnp.where(out_own, 1, 0)
    place_count = jnp.where(diag, 3 + 4 * (3 - k), 1) + jnp.where(below, 8, 0)
    pl.semaphore_wait(barrier, 7 + 3 + 8 + 16 - own_count + place_count)

    each(8, lambda i: send(im_src.at[i], im_rs.at[y], S_IR + i, R_IR, device(x, i, z, c), i == y))

    my_rows = pl.ds(pl.multiple_of(c * 256, 256), 256)
    keep = pl.ds(pl.multiple_of(c * 1024, 1024), 1024)
    give = pl.ds(pl.multiple_of((1 - c) * 1024, 1024), 1024)
    partner = device(x, y, z, 1 - c)

    @pl.when(works)
    def _():
        send(factor.at[:, give], fraw.at[my_rows, :], S_FX, R_FX, partner)
        pltpu.make_async_copy(factor.at[:, keep], fraw.at[my_rows, :], rsem.at[R_FX]).start()

    arrived(im_rs, R_IR)
    total = ((im_rs[0] + im_rs[1]) + (im_rs[2] + im_rs[3])) + (
        (im_rs[4] + im_rs[5]) + (im_rs[6] + im_rs[7]))
    ag_src[...] = (total / 65536.0).astype(BF16).astype(F32)
    each(8, lambda i: send(ag_src, im_ag.at[y], S_IG + i, R_IG, device(x, i, z, c), i == y))

    @pl.when(works)
    def _():
        arrived(fraw, R_FX)
        raw = fraw[...]
        high = raw.astype(BF16)
        fhigh[...] = high
        flow[...] = (raw - high.astype(F32)).astype(BF16)

    arrived(im_ag, R_IG)
    for i in range(8):
        im_low[:, i * 128:(i + 1) * 128] = im_ag[i].astype(BF16)

    t_src[...] = lax.dot_general(im_low[...], kmat[:, give], NN, preferred_element_type=F32)
    send(t_src, t_rc, S_TC, R_TC, partner)
    mine = lax.dot_general(im_low[...], kmat[:, keep], NN, preferred_element_type=F32)
    arrived(t_rc, R_TC)
    mine = mine + t_rc[...]
    for i in range(8):
        rs_src[i] = mine[:, i * 128:(i + 1) * 128]

    def piece_dev(i, to):
        zt, ht, ct = 4 * h + 2 * c + i // 4, i // 2 % 2, i % 2
        own = (to == x) & (zt == z) & (ht == h) & (ct == c)
        return device(to, 2 * k + ht, zt, ct), own

    def scatter(src, dst, s, r, to):
        def one(i):
            dev, own = piece_dev(i, to)
            send(src.at[i], dst, s + i, r, dev, own)
        each(8, one)

    def eight(buf, *lead):
        v = [buf[(*lead, i)] for i in range(8)]
        return ((v[0] + v[1]) + (v[2] + v[3])) + ((v[4] + v[5]) + (v[6] + v[7]))

    scatter(rs_src, rs_t.at[z], S_RT, R_RT, x)
    arrived(rs_t, R_RT)
    x_src[...] = eight(rs_t)

    @pl.when(jnp.logical_not(diag))
    def _():
        send(x_src, x_buf.at[(x - k + 3) % 4], S_X, R_X, device(k, y, z, c))

    def slab_dev(i):
        own = (i // 2 == h) & (i % 2 == c)
        return device(x, 2 * k + i // 2, z, i % 2), own

    @pl.when(diag)
    def _():
        arrived(x_buf, R_X)
        s_src[...] = (x_src[...] + x_buf[0]) + (x_buf[1] + x_buf[2])
        for j in range(3):
            @pl.when(j < k)
            def _():
                arrived(rs_ab.at[j], R_AB + j)
                s_src[...] -= eight(rs_ab, j)
        each(4, lambda i: send(s_src, inp.at[2 * h + c], S_G + i, R_IN, *slab_dev(i)))

    @pl.when(works)
    def _():
        arrived(inp, R_IN)
        v = jnp.concatenate([inp[i] for i in range(4)], axis=1)
        high = v.astype(BF16)
        both = jnp.concatenate([high, (v - high.astype(F32)).astype(BF16)], axis=0)
        prod = lax.dot_general(both, fhigh[...], NN, preferred_element_type=F32)
        rest = lax.dot_general(high, flow[...], NN, preferred_element_type=F32)
        part = prod[0:32] + (prod[32:64] + rest)
        for i in range(8):
            ab_src[i] = part[:, i * 128:(i + 1) * 128]
        scatter(ab_src, rs_ab.at[x, z], S_RA, R_AB + x, k)

    def later_dev(i):
        return device(x, 2 * (k + 1) + i // 2, z, i % 2)

    @pl.when(diag)
    def _():
        arrived(rs_ab.at[k], R_AB + k)
        u_src[...] = eight(rs_ab, k)
        each(4 * (3 - k), lambda i: send(u_src, inp.at[2 * h + c], S_B + i, R_IN, later_dev(i)))
        each(3, lambda i: send(u_src, u_src, S_O1 + i, R_O1, device((x + 1 + i) % 4, y, z, c)))

    @pl.when(jnp.logical_not(diag))
    def _():
        arrived(u_src, R_O1)

    def out_dev(i):
        own = out_own & (i // 2 == z) & (i % 2 == c)
        return device(x, 2 * k + z // 4, i // 2, i % 2), own

    slot = (z % 4) * 4 + 2 * h + c
    each(16, lambda i: send(u_src, o_buf.at[slot], S_O2 + i, R_O2, *out_dev(i)))
    arrived(o_buf, R_O2)
    for i in range(16):
        out[:, i * 128:(i + 1) * 128] = o_buf[i]

    each(8, lambda i: sent(im_src.at[i], S_IR + i, device(x, i, z, c), i == y))
    each(8, lambda i: sent(ag_src, S_IG + i, device(x, i, z, c), i == y))
    sent(t_src, S_TC, partner)

    def scattered(src, s, to):
        def one(i):
            dev, own = piece_dev(i, to)
            sent(src.at[i], s + i, dev, own)
        each(8, one)
    scattered(rs_src, S_RT, x)

    @pl.when(works)
    def _():
        sent(factor.at[:, give], S_FX, partner)
        scattered(ab_src, S_RA, k)

    @pl.when(jnp.logical_not(diag))
    def _():
        sent(x_src, S_X, device(k, y, z, c))

    @pl.when(diag)
    def _():
        each(4, lambda i: sent(s_src, S_G + i, *slab_dev(i)))
        each(4 * (3 - k), lambda i: sent(u_src, S_B + i, later_dev(i)))
        each(3, lambda i: sent(u_src, S_O1 + i, device((x + 1 + i) % 4, y, z, c)))
    each(16, lambda i: sent(u_src, S_O2 + i, *out_dev(i)))


def body(points, centres, vector, factor):
    def piece(*lead):
        return pltpu.VMEM((*lead, 32, 128), F32)

    any_space = pl.BlockSpec(memory_space=pl.ANY)
    return pl.pallas_call(
        sweep_kernel,
        out_shape=jax.ShapeDtypeStruct((32, 2048), F32),
        in_specs=[any_space] * 4,
        out_specs=pl.BlockSpec(memory_space=pltpu.VMEM),
        scratch_shapes=[
            pltpu.VMEM((1024, 512), BF16), pltpu.VMEM((2048, 512), BF16), pltpu.VMEM((32, 2048), F32),
            pltpu.VMEM((1, 2048), F32), pltpu.VMEM((1024, 2048), BF16),
            pltpu.VMEM((512, 1024), F32), pltpu.VMEM((512, 1024), BF16), pltpu.VMEM((512, 1024), BF16),
            piece(8), piece(8), piece(), piece(8), pltpu.VMEM((32, 1024), BF16),
            pltpu.VMEM((32, 1024), F32), pltpu.VMEM((32, 1024), F32), piece(8), piece(8), piece(), piece(3),
            piece(), piece(4), piece(8), piece(4, 8), piece(), piece(16),
            pltpu.SemaphoreType.DMA((S_END,)), pltpu.SemaphoreType.DMA((R_END,)),
        ],
        compiler_params=pltpu.CompilerParams(
            collective_id=0, has_side_effects=True, vmem_limit_bytes=48 * 2**20),
        cost_estimate=pl.CostEstimate(
            flops=2 * 1024 * 2048 * 512, bytes_accessed=6 * 2**20, transcendentals=1024 * 2048),
    )(points, centres, vector, factor)


def solution(mesh):
    placed = (P("pts", None), P("ctr", None), P(None, "ctr"), P("pts", "ctr"))
    return jax.shard_map(
        body, mesh=mesh, in_specs=placed, out_specs=P(None, "ctr"), check_vma=False
    )
```

time: 1800 us -> 131 us (0.07)
  waiting for transfers between devices: 1610 us -> 0 us
  blocking collectives: 141 us -> 0 us
  Pallas kernels: 0 us -> 125 us
  matrix products: 22.9 us -> 0 us
    psum x9 -> x0, waiting for transfers between devices: 1610 us -> none  [the longest x4 765 us: body(): solved = lax.psum(spread(rows_part), 'pts')]
    psum x7 -> x0, blocking collectives: 141 us -> none  [broadcast(): return lax.psum(jnp.where(mine, x, jnp.zeros_like(x)), axis)]
    pallas_call x0 -> x1, Pallas kernels: none -> 125 us  [body(): pl.pallas_call(sweep_kernel, out_shape=jax.ShapeDtypeStruct((32, 2048), F...]
    dot_general x10 -> x0, matrix products: 22.9 us -> none  [the longest x7 14 us: spread(): jnp.dot(row_values, factor, precision=lax.Precision.HIGHEST, preferred_el...]
  transfers between devices with their start and end apart: 9 -> 0, of which waited for: 9 -> 0; matrix products, arithmetic and copies ran while one was open for 0% -> 0% of each run, Pallas kernels for 0% -> 0%
where the time goes in v1:
time: 131 us
  Pallas kernels  125 us (95%)
  local copies, waits for them, and re-layouts  6.06 us (5%)
    pallas_call x1, Pallas kernels, body(): pl.pallas_call(sweep_kernel, out_shape=jax.ShapeDtypeStruct((32, 2048), F...  125 us
    unnamed x9, local copies, waits for them, and re-layouts  6.06 us

profile of v1, /device:TPU:57, one launch (start us, length us, event | category | flops | bytes accessed | tf_op | source)
XLA Modules:
  0.0 131.0 jit_solution(17062253412714896301)
XLA Ops:
  0.0 0.0 copy-start
  0.0 1.6 %copy-done = bf16[2048,512]{1,0:T(8,128)(2,1)S(1)} copy-done((bf16[2048,512]{1,0:T(8,128)(2,1)S(1)}, bf16[2048,512]{1,0:T(8,128)(2,1)}, u32[]{:S(2)}) %copy-start) | copy-done | bytes 2097176
  1.6 0.0 copy-start.1
  1.6 1.6 %copy-done.1 = f32[256,2048]{1,0:T(8,128)S(1)} copy-done((f32[256,2048]{1,0:T(8,128)S(1)}, f32[256,2048]{1,0:T(8,128)}, u32[]{:S(2)}) %copy-start.1) | copy-done | bytes 2097176
  3.2 0.0 copy-start.2
  3.2 1.2 copy-done.2
  4.4 0.0 copy-start.3
  4.4 0.9 copy-done.3
  5.4 124.9 %shard_map.46 = f32[32,2048]{1,0:T(8,128)S(1)} custom-call(bf16[1024,512]{1,0:T(8,128)(2,1)S(1)} %copy-done.2, bf16[2048,512]{1,0:T(8,128)(2,1)S(1)} %copy-done, f32[32,2048]{1,0:T(8,128)S(1)} %copy-done.3, f32[256,2048]{1,0:T(8,128)S(1)} %copy-done.1), custom_call_target="tpu_custom_call" | custom-call | flops 2147483648 | bytes 6291456 | tf_op jit(solution)/shard_map/pallas_call | solution.py:281
  130.2 0.7 copy.6
Async XLA Ops:
  0.0 1.6 %copy-start = (bf16[2048,512]{1,0:T(8,128)(2,1)S(1)}, bf16[2048,512]{1,0:T(8,128)(2,1)}, u32[]{:S(2)}) copy-start(bf16[2048,512]{1,0:T(8,128)(2,1)} %centres.1) | copy-start | bytes 6291460
  1.6 1.6 %copy-start.1 = (f32[256,2048]{1,0:T(8,128)S(1)}, f32[256,2048]{1,0:T(8,128)}, u32[]{:S(2)}) copy-start(f32[256,2048]{1,0:T(8,128)} %factor.1) | copy-start | bytes 6291460
  3.2 1.2 copy-start.2
  4.4 0.9 copy-start.3

commit v2 on v1

v2 whole, which is shorter than its diff:
```python
import jax
import jax.numpy as jnp
from jax import lax
from jax.experimental import pallas as pl
from jax.experimental.pallas import tpu as pltpu
from jax.sharding import PartitionSpec as P

F32, BF16 = jnp.float32, jnp.bfloat16
MESH = pl.DeviceIdType.MESH
NN = (((1,), (0,)), ((), ()))
NT = (((1,), (1,)), ((), ()))
PT = 256
AROUND = (4, 3, 5, 2, 6, 1, 7)
S_IR, S_IG, S_TC, S_FX, S_RT, S_X, S_G, S_RA, S_B, S_O1, S_O2, S_O3, S_END = (
    0, 8, 16, 17, 18, 26, 27, 31, 39, 51, 55, 71, 72)
(R_IR, R_IG, R_TC, R_FX, R_RT, R_X, R_IN, R_AB, R_O1, R_O2, R_O3, L_C, L_P, L_V, R_END) = (
    0, 1, 2, 3, 4, 5, 6, 7, 11, 12, 13, 14, 15, 16, 17)


def device(x, y, z, c):
    return ((x * 8 + z) * 2 + c, y)


def sweep_kernel(
    points, centres, vector, factor, out,
    pts, cen, vec, norm_row, kmat, fraw, fhigh, flow,
    im_src, im_rs, ag_src, im_ag, im_low, t_src, t_rc, rs_src, rs_t, x_src, x_buf,
    s_src, inp, ab_src, rs_ab, u_src, o_buf, ssem, rsem,
):
    p, y = lax.axis_index("pts"), lax.axis_index("ctr")
    x, z, c = p // 16, (p // 2) % 8, p % 2
    k, h = y // 2, y % 2
    diag, works, below, last = x == k, x <= k, x < k, k == 3

    pending = []

    def send(src, dst, s, r, dev, when=None, like=None):
        def start():
            pltpu.make_async_remote_copy(
                src_ref=src, dst_ref=dst, send_sem=ssem.at[s], recv_sem=rsem.at[r],
                device_id=dev, device_id_type=MESH).start()

        def sent():
            buf = src if like is None else like()
            pltpu.make_async_copy(buf, buf, ssem.at[s]).wait()
        if when is None:
            start()
            pending.append(sent)
        else:
            pl.when(when)(start)
            pending.append(lambda: pl.when(when)(sent))

    def nested(first, when):
        inner = pending[first:]
        del pending[first:]

        def waits():
            for wait in inner:
                wait()
        pending.append(lambda: pl.when(when)(waits))

    def stay(src, dst, r):
        pltpu.make_async_copy(src, dst, rsem.at[r]).start()

    def arrived(buf, r):
        pltpu.make_async_copy(buf, buf, rsem.at[r]).wait()

    def each(n, f):
        def step(i, carry):
            f(i)
            return carry
        lax.fori_loop(0, n, step, 0)

    load_c = pltpu.make_async_copy(centres, cen, rsem.at[L_C])
    load_p = pltpu.make_async_copy(points, pts, rsem.at[L_P])
    load_v = pltpu.make_async_copy(vector, vec, rsem.at[L_V])
    load_c.start()
    load_p.start()
    load_v.start()

    barrier = pltpu.get_barrier_semaphore()

    def greet(dev):
        pl.semaphore_signal(barrier, inc=1, device_id=dev, device_id_type=MESH)

    each(7, lambda i: greet(device(x, (y + 1 + i) % 8, z, c)))
    each(3, lambda i: greet(device(x, 2 * k + (h + (i + 1) // 2) % 2, z, (c + (i + 1) % 2) % 2)))
    rs_own = z // 2 == 2 * h + c
    rs_y, rs_c = 2 * k + z // 4, (z // 2) % 2

    def greet_rs(i):
        @pl.when(jnp.logical_not(rs_own & (i == z)))
        def _():
            greet(device(x, rs_y, i, rs_c))
    each(8, greet_rs)

    def greet_out(i):
        dev = (2 * k + i // 2 % 2, 4 * h + i // 4, i % 2)

        @pl.when(jnp.logical_not((dev[0] == y) & (dev[1] == z) & (dev[2] == c)))
        def _():
            greet(device(x, *dev))
    pl.when(jnp.logical_not(last))(lambda: each(16, greet_out))
    pl.when(last)(lambda: each(7, lambda i: greet(device(x, y, (z + 1 + i) % 8, c))))
    out_own = z // 4 == h
    rs_away, out_away = jnp.logical_not(rs_own), jnp.logical_not(out_own)
    off_diag, not_last = jnp.logical_not(diag), jnp.logical_not(last)
    plain = diag & last
    dealt = works & jnp.logical_not(plain)
    ab_own = rs_own & diag
    ab_away = jnp.logical_not(ab_own)
    more = [k + 1 + j <= 3 for j in range(3)]

    @pl.when(diag)
    def _():
        each(3, lambda i: greet(device((x + 1 + i) % 4, y, z, c)))
        each(8 * k, lambda i: greet(device(i // 8, rs_y, i % 8, rs_c)))

    @pl.when(jnp.logical_not(diag))
    def _():
        greet(device(k, y, z, c))

    @pl.when(below)
    def _():
        each(4, lambda i: greet(device(x, 2 * x + i // 2, z, i % 2)))

    load_c.wait()
    squares = jnp.square(cen[...].astype(F32))
    folded = (squares[:, 0:128] + squares[:, 128:256]) + (squares[:, 256:384] + squares[:, 384:512])
    norm_row[...] = jnp.sum(folded.T, axis=0, keepdims=True) * (1.0 / 64.0)
    load_p.wait()
    load_v.wait()

    def kernel_step(i):
        rows = pl.ds(pl.multiple_of(i * PT, PT), PT)
        pt = pts[rows, :]
        prods = lax.dot_general(pt, cen[...], NT, preferred_element_type=F32)
        norms = jnp.sum(jnp.square(pt.astype(F32)), axis=1, keepdims=True) * (1.0 / 64.0)
        kern = jnp.exp(prods * (1.0 / 32.0) - (norms + norm_row[...])).astype(BF16)
        kmat[rows, :] = kern
        images = lax.dot_general(vec[...].astype(BF16), kern, NT, preferred_element_type=F32)
        im_src[2 * i] = images[:, 0:128]
        im_src[2 * i + 1] = images[:, 128:256]
    each(4, kernel_step)

    scatter_count = 8 - jnp.where(rs_own, 1, 0)
    result_count = jnp.where(last, 7, 16 - jnp.where(out_own, 1, 0))
    place_count = jnp.where(diag, 3 + 4 * (3 - k), 1) + jnp.where(below, 8, 0)
    pl.semaphore_wait(barrier, 7 + 3 + scatter_count + result_count + place_count)

    def phase_images():
        for n, d in enumerate(AROUND):
            i = (y + d) % 8
            send(im_src.at[i], im_rs.at[y], S_IR + n, R_IR, device(x, i, z, c), like=lambda: im_src.at[0])
        stay(im_src.at[y], im_rs.at[y], R_IR)

    my_rows = pl.ds(pl.multiple_of(c * 256, 256), 256)
    keep = pl.ds(pl.multiple_of(c * 1024, 1024), 1024)
    give = pl.ds(pl.multiple_of((1 - c) * 1024, 1024), 1024)
    partner = device(x, y, z, 1 - c)

    def phase_factor():
        send(factor.at[:, give], fraw.at[my_rows, :], S_FX, R_FX, partner, works, lambda: fraw.at[0:256, :])

        @pl.when(works)
        def _():
            stay(factor.at[:, keep], fraw.at[my_rows, :], R_FX)

    def phase_split():
        @pl.when(works)
        def _():
            arrived(fraw, R_FX)
            raw = fraw[...]
            high = raw.astype(BF16)
            fhigh[...] = high
            flow[...] = (raw - high.astype(F32)).astype(BF16)

    def eight(buf, *lead):
        v = [buf[(*lead, i)] for i in range(8)]
        return ((v[0] + v[1]) + (v[2] + v[3])) + ((v[4] + v[5]) + (v[6] + v[7]))

    def phase_rounded():
        arrived(im_rs, R_IR)
        ag_src[...] = (eight(im_rs) / 65536.0).astype(BF16).astype(F32)
        for n, d in enumerate(AROUND):
            send(ag_src, im_ag.at[y], S_IG + n, R_IG, device(x, (y + d) % 8, z, c))
        stay(ag_src, im_ag.at[y], R_IG)

        arrived(im_ag, R_IG)
        for i in range(8):
            im_low[:, i * 128:(i + 1) * 128] = im_ag[i].astype(BF16)

    def piece(b):
        zb, hb, cb = (z + b // 4) % 2, (h + b // 2 % 2) % 2, (c + b % 2) % 2
        return 4 * zb + 2 * hb + cb, (2 * k + hb, 4 * h + 2 * c + zb, cb)

    def scatter(src, dst, s, r, to, own, away, bits):
        for b in bits:
            g, place = piece(b)
            send(src.at[g], dst, s + b, r, device(to, *place), None if b else away, lambda: src.at[0])
            if not b:
                pl.when(own)(lambda: stay(src.at[g], dst, r))

    def phase_totals():
        t_src[...] = lax.dot_general(im_low[...], kmat[:, give], NN, preferred_element_type=F32)
        send(t_src, t_rc, S_TC, R_TC, partner)
        mine = lax.dot_general(im_low[...], kmat[:, keep], NN, preferred_element_type=F32)
        arrived(t_rc, R_TC)
        mine = mine + t_rc[...]
        for i in range(8):
            rs_src[i] = mine[:, i * 128:(i + 1) * 128]
        scatter(rs_src, rs_t.at[z], S_RT, R_RT, x, rs_own, rs_away, (7, 6, 5, 4, 3, 2, 1, 0))

    def phase_across():
        arrived(rs_t, R_RT)
        x_src[...] = eight(rs_t)
        send(x_src, x_buf.at[(x - k + 3) % 4], S_X, R_X, device(k, y, z, c), off_diag)

    def phase_residual():
        @pl.when(diag)
        def _():
            first = len(pending)
            arrived(x_buf, R_X)
            s_src[...] = (x_src[...] + x_buf[0]) + (x_buf[1] + x_buf[2])
            for j in range(3):
                @pl.when(j < k)
                def _():
                    arrived(rs_ab.at[j], R_AB + j)
                    s_src[...] -= eight(rs_ab, j)
            for n in (3, 2, 1):
                send(s_src, inp.at[2 * h + c], S_G + n, R_IN,
                     device(x, 2 * k + (h + n // 2) % 2, z, (c + n % 2) % 2))
            stay(s_src, inp.at[2 * h + c], R_IN)
            nested(first, diag)

    def phase_product():
        @pl.when(works)
        def _():
            first = len(pending)
            arrived(inp, R_IN)
            v = jnp.concatenate([inp[i] for i in range(4)], axis=1)
            high = v.astype(BF16)
            both = jnp.concatenate([high, (v - high.astype(F32)).astype(BF16)], axis=0)
            far = jnp.where(plain, (z // 4 + 1) % 2, (z + 1) % 2) * 4
            for own_half in range(2):
                start = far + own_half * (4 - 2 * far)
                cols = pl.ds(pl.multiple_of(start * 128, 512), 512)
                prod = lax.dot_general(both, fhigh[:, cols], NN, preferred_element_type=F32)
                rest = lax.dot_general(high, flow[:, cols], NN, preferred_element_type=F32)
                part = prod[0:32] + (prod[32:64] + rest)
                for i in range(4):
                    ab_src[start + i] = part[:, i * 128:(i + 1) * 128]

                @pl.when(plain)
                def _():
                    inside = len(pending)
                    for n in range(4):
                        g = start + (z + 2 + n) % 4
                        if own_half and n == 2:
                            stay(ab_src.at[g], rs_ab.at[x, z], R_AB + x)
                        else:
                            send(ab_src.at[g], rs_ab.at[x, z], S_RA + 4 * own_half + n, R_AB + x,
                                 device(x, y, g, c), None, lambda: ab_src.at[0])
                    nested(inside, plain)

                @pl.when(dealt)
                def _():
                    inside = len(pending)
                    bits = (3, 2, 1, 0) if own_half else (7, 6, 5, 4)
                    scatter(ab_src, rs_ab.at[x, z], S_RA, R_AB + x, k, ab_own, ab_away, bits)
                    nested(inside, dealt)
            nested(first, works)

    def phase_solved():
        @pl.when(diag)
        def _():
            first = len(pending)
            arrived(rs_ab.at[k], R_AB + k)
            u_src[...] = eight(rs_ab, k)
            for j in range(3):
                for n in range(4):
                    send(u_src, inp.at[2 * h + c], S_B + 4 * j + n, R_IN,
                         device(x, (2 * (k + 1 + j) + n // 2) % 8, z, n % 2), more[j])
            for n in range(3):
                send(u_src, u_src, S_O1 + n, R_O1, device((x + 1 + n) % 4, y, z, c))
            nested(first, diag)

        @pl.when(jnp.logical_not(diag))
        def _():
            arrived(u_src, R_O1)

    def phase_results():
        @pl.when(not_last)
        def _():
            first = len(pending)
            slot = (z % 4) * 4 + 2 * h + c
            for n, d in enumerate(AROUND):
                for e in range(2):
                    zt = (z + d) % 8
                    send(u_src, o_buf.at[slot], S_O2 + 2 * n + e, R_O2, device(x, 2 * k + z // 4, zt, (c + e) % 2))
            send(u_src, o_buf.at[slot], S_O2 + 14, R_O2, device(x, 2 * k + z // 4, z, 1 - c))
            send(u_src, o_buf.at[slot], S_O2 + 15, R_O2, device(x, 2 * k + z // 4, z, c), out_away)

            @pl.when(out_own)
            def _():
                stay(u_src, o_buf.at[slot], R_O2)
            arrived(o_buf, R_O2)
            nested(first, not_last)

        @pl.when(last)
        def _():
            first = len(pending)
            slot = c * 8 + z
            for n, d in enumerate(AROUND):
                send(u_src, o_buf.at[slot], S_O2 + n, R_O2, device(x, y, (z + d) % 8, c))
            stay(u_src, o_buf.at[slot], R_O2)
            mine = o_buf.at[pl.ds(c * 8, 8)]
            arrived(mine, R_O2)
            send(mine, mine, S_O3, R_O3, partner, None, lambda: o_buf.at[0:8])
            arrived(o_buf.at[pl.ds(8 - c * 8, 8)], R_O3)
            nested(first, last)
        for i in range(16):
            out[:, i * 128:(i + 1) * 128] = o_buf[i]

    phases = (phase_images, phase_factor, phase_rounded, phase_totals, phase_across, phase_split, phase_residual,
              phase_product, phase_solved, phase_results)
    for phase in phases:
        phase()
    for wait in pending:
        wait()


def body(points, centres, vector, factor):
    def piece(*lead):
        return pltpu.VMEM((*lead, 32, 128), F32)

    any_space = pl.BlockSpec(memory_space=pl.ANY)
    return pl.pallas_call(
        sweep_kernel,
        out_shape=jax.ShapeDtypeStruct((32, 2048), F32),
        in_specs=[any_space] * 4,
        out_specs=pl.BlockSpec(memory_space=pltpu.VMEM),
        scratch_shapes=[
            pltpu.VMEM((1024, 512), BF16), pltpu.VMEM((2048, 512), BF16), pltpu.VMEM((32, 2048), F32),
            pltpu.VMEM((1, 2048), F32), pltpu.VMEM((1024, 2048), BF16),
            pltpu.VMEM((512, 1024), F32), pltpu.VMEM((512, 1024), BF16), pltpu.VMEM((512, 1024), BF16),
            piece(8), piece(8), piece(), piece(8), pltpu.VMEM((32, 1024), BF16),
            pltpu.VMEM((32, 1024), F32), pltpu.VMEM((32, 1024), F32), piece(8), piece(8), piece(), piece(3),
            piece(), piece(4), piece(8), piece(4, 8), piece(), piece(16),
            pltpu.SemaphoreType.DMA((S_END,)), pltpu.SemaphoreType.DMA((R_END,)),
        ],
        compiler_params=pltpu.CompilerParams(
            collective_id=0, has_side_effects=True, vmem_limit_bytes=60 * 2**20),
        cost_estimate=pl.CostEstimate(
            flops=2 * 1024 * 2048 * 512, bytes_accessed=6 * 2**20, transcendentals=1024 * 2048),
    )(points, centres, vector, factor)


def solution(mesh):
    placed = (P("pts", None), P("ctr", None), P(None, "ctr"), P("pts", "ctr"))
    return jax.shard_map(
        body, mesh=mesh, in_specs=placed, out_specs=P(None, "ctr"), check_vma=False
    )
```

time: 131 us -> 122 us (0.931)
  Pallas kernels: 125 us -> 120 us
  local copies, waits for them, and re-layouts: 6.06 us -> 1.67 us
    pallas_call x1, Pallas kernels: 125 us -> 120 us  [body(): pl.pallas_call(sweep_kernel, out_shape=jax.ShapeDtypeStruct((32, 2048), F...]
    unnamed x9 -> x1, local copies, waits for them, and re-layouts: 6.06 us -> 1.67 us
where the time goes in v2:
time: 122 us
  Pallas kernels  120 us (98%)
  local copies, waits for them, and re-layouts  1.67 us (1%)
    pallas_call x1, Pallas kernels, body(): pl.pallas_call(sweep_kernel, out_shape=jax.ShapeDtypeStruct((32, 2048), F...  120 us

profile of v2, /device:TPU:57, one launch (start us, length us, event | category | flops | bytes accessed | tf_op | source)
XLA Modules:
  0.0 121.5 jit_solution(2081390053483060577)
XLA Ops:
  0.0 119.8 %shard_map.46 = f32[32,2048]{1,0:T(8,128)} custom-call(bf16[1024,512]{1,0:T(8,128)(2,1)} %points.1, bf16[2048,512]{1,0:T(8,128)(2,1)} %centres.1, f32[32,2048]{1,0:T(8,128)} %vector.1, f32[256,2048]{1,0:T(8,128)} %factor.1), custom_call_target="tpu_custom_call" | custom-call | flops 2147483648 | bytes 6291456 | tf_op jit(solution)/shard_map/pallas_call | solution.py:338
  119.8 1.7 %copy.6 = f32[32,2048]{1,0:T(8,128)} copy(f32[32,2048]{1,0:T(8,128)} %shard_map.46) | data formatting | bytes 524288

commit v3 on v2

--- a/solution.py
+++ b/solution.py
@@ -12,9 +12,9 @@
 PT = 256
 AROUND = (4, 3, 5, 2, 6, 1, 7)
 S_IR, S_IG, S_TC, S_FX, S_RT, S_X, S_G, S_RA, S_B, S_O1, S_O2, S_O3, S_END = (
-    0, 8, 16, 17, 18, 26, 27, 31, 39, 51, 55, 71, 72)
-(R_IR, R_IG, R_TC, R_FX, R_RT, R_X, R_IN, R_AB, R_O1, R_O2, R_O3, L_C, L_P, L_V, R_END) = (
-    0, 1, 2, 3, 4, 5, 6, 7, 11, 12, 13, 14, 15, 16, 17)
+    0, 14, 28, 29, 30, 38, 42, 46, 54, 66, 70, 86, 87)
+(R_IR, R_IG, R_TC, R_FX, R_RT, R_X, R_IN, R_AB, R_O1, R_O2, R_O3, R_XQ, L_C, L_P, L_V, L_O, R_END) = (
+    0, 2, 4, 5, 6, 7, 8, 9, 13, 14, 15, 16, 17, 18, 19, 20, 21)
 
 
 def device(x, y, z, c):
@@ -23,14 +23,15 @@
 
 def sweep_kernel(
     points, centres, vector, factor, out,
-    pts, cen, vec, norm_row, kmat, fraw, fhigh, flow,
-    im_src, im_rs, ag_src, im_ag, im_low, t_src, t_rc, rs_src, rs_t, x_src, x_buf,
-    s_src, inp, ab_src, rs_ab, u_src, o_buf, ssem, rsem,
+    pts, cen, vec, vec_low, norm_row, kmat, fraw, fhigh, flow,
+    im_src, im_rs, ag_src, im_ag, im_low, t_keep, t_src, t_rc, rs_src, rs_t, x_src, x_buf,
+    s_src, inp, ab_src, rs_ab, u_src, o_buf, x_quad, out_vm, ssem, rsem,
 ):
     p, y = lax.axis_index("pts"), lax.axis_index("ctr")
     x, z, c = p // 16, (p // 2) % 8, p % 2
     k, h = y // 2, y % 2
     diag, works, below, last = x == k, x <= k, x < k, k == 3
+    first_pair = k == 0
 
     pending = []
 
@@ -103,6 +104,9 @@
     pl.when(jnp.logical_not(last))(lambda: each(16, greet_out))
     pl.when(last)(lambda: each(7, lambda i: greet(device(x, y, (z + 1 + i) % 8, c))))
     out_own = z // 4 == h
+    later_pair = jnp.logical_not(first_pair)
+    fed = jnp.logical_not(diag & first_pair)
+    later_diag = diag & later_pair
     rs_away, out_away = jnp.logical_not(rs_own), jnp.logical_not(out_own)
     off_diag, not_last = jnp.logical_not(diag), jnp.logical_not(last)
     plain = diag & last
@@ -113,7 +117,13 @@
 
     @pl.when(diag)
     def _():
-        each(3, lambda i: greet(device((x + 1 + i) % 4, y, z, c)))
+        @pl.when(first_pair)
+        def _():
+            each(12, lambda i: greet(device(1 + i // 4, i // 2 % 2, z, i % 2)))
+
+        @pl.when(jnp.logical_not(first_pair))
+        def _():
+            each(3, lambda i: greet(device((x + 1 + i) % 4, y, z, c)))
         each(8 * k, lambda i: greet(device(i // 8, rs_y, i % 8, rs_c)))
 
     @pl.when(jnp.logical_not(diag))
@@ -130,29 +140,41 @@
     norm_row[...] = jnp.sum(folded.T, axis=0, keepdims=True) * (1.0 / 64.0)
     load_p.wait()
     load_v.wait()
+    vec_low[...] = vec[...].astype(BF16)
 
     def kernel_step(i):
-        rows = pl.ds(pl.multiple_of(i * PT, PT), PT)
+        rows = pl.ds(i * PT, PT)
         pt = pts[rows, :]
         prods = lax.dot_general(pt, cen[...], NT, preferred_element_type=F32)
         norms = jnp.sum(jnp.square(pt.astype(F32)), axis=1, keepdims=True) * (1.0 / 64.0)
         kern = jnp.exp(prods * (1.0 / 32.0) - (norms + norm_row[...])).astype(BF16)
         kmat[rows, :] = kern
-        images = lax.dot_general(vec[...].astype(BF16), kern, NT, preferred_element_type=F32)
-        im_src[2 * i] = images[:, 0:128]
-        im_src[2 * i + 1] = images[:, 128:256]
-    each(4, kernel_step)
+        images = lax.dot_general(vec_low[...], kern, NT, preferred_element_type=F32)
+        for r in range(2):
+            for j in range(2):
+                im_src[i // 2, 4 * r + 2 * (i % 2) + j] = images[16 * r:16 * r + 16, 128 * j:128 * j + 128]
+
+    kernel_step(0)
+    kernel_step(1)
 
     scatter_count = 8 - jnp.where(rs_own, 1, 0)
     result_count = jnp.where(last, 7, 16 - jnp.where(out_own, 1, 0))
-    place_count = jnp.where(diag, 3 + 4 * (3 - k), 1) + jnp.where(below, 8, 0)
+    place_count = jnp.where(diag, 3 + 4 * (3 - k), jnp.where(first_pair, 4, 1)) + jnp.where(below, 8, 0)
     pl.semaphore_wait(barrier, 7 + 3 + scatter_count + result_count + place_count)
 
-    def phase_images():
+    def send_images(half):
         for n, d in enumerate(AROUND):
             i = (y + d) % 8
-            send(im_src.at[i], im_rs.at[y], S_IR + n, R_IR, device(x, i, z, c), like=lambda: im_src.at[0])
-        stay(im_src.at[y], im_rs.at[y], R_IR)
+            send(im_src.at[half, i], im_rs.at[half, y], S_IR + 7 * half + n, R_IR + half, device(x, i, z, c),
+                 like=lambda: im_src.at[0, 0])
+        stay(im_src.at[half, y], im_rs.at[half, y], R_IR + half)
+
+    def phase_images():
+        send_images(0)
+        phase_factor()
+        kernel_step(2)
+        kernel_step(3)
+        send_images(1)
 
     my_rows = pl.ds(pl.multiple_of(c * 256, 256), 256)
     keep = pl.ds(pl.multiple_of(c * 1024, 1024), 1024)
@@ -180,15 +202,13 @@
         return ((v[0] + v[1]) + (v[2] + v[3])) + ((v[4] + v[5]) + (v[6] + v[7]))
 
     def phase_rounded():
-        arrived(im_rs, R_IR)
-        ag_src[...] = (eight(im_rs) / 65536.0).astype(BF16).astype(F32)
-        for n, d in enumerate(AROUND):
-            send(ag_src, im_ag.at[y], S_IG + n, R_IG, device(x, (y + d) % 8, z, c))
-        stay(ag_src, im_ag.at[y], R_IG)
-
-        arrived(im_ag, R_IG)
-        for i in range(8):
-            im_low[:, i * 128:(i + 1) * 128] = im_ag[i].astype(BF16)
+        for half in range(2):
+            arrived(im_rs.at[half], R_IR + half)
+            ag_src[half] = (eight(im_rs, half) / 65536.0).astype(BF16).astype(F32)
+            for n, d in enumerate(AROUND):
+                send(ag_src.at[half], im_ag.at[half, y], S_IG + 7 * half + n, R_IG + half,
+                     device(x, (y + d) % 8, z, c))
+            stay(ag_src.at[half], im_ag.at[half, y], R_IG + half)
 
     def piece(b):
         zb, hb, cb = (z + b // 4) % 2, (h + b // 2 % 2) % 2, (c + b % 2) % 2
@@ -202,9 +222,20 @@
                 pl.when(own)(lambda: stay(src.at[g], dst, r))
 
     def phase_totals():
-        t_src[...] = lax.dot_general(im_low[...], kmat[:, give], NN, preferred_element_type=F32)
+        for half in range(2):
+            arrived(im_ag.at[half], R_IG + half)
+            for i in range(8):
+                im_low[16 * (i // 4):16 * (i // 4) + 16, 512 * half + 128 * (i % 4):512 * half + 128 * (i % 4) + 128] = (
+                    im_ag[half, i].astype(BF16))
+            rows = pl.ds(512 * half, 512)
+            low = im_low[:, 512 * half:512 * half + 512]
+            theirs = lax.dot_general(low, kmat[rows, give], NN, preferred_element_type=F32)
+            if half == 0:
+                t_src[...] = theirs
+                t_keep[...] = lax.dot_general(low, kmat[rows, keep], NN, preferred_element_type=F32)
+        t_src[...] += theirs
         send(t_src, t_rc, S_TC, R_TC, partner)
-        mine = lax.dot_general(im_low[...], kmat[:, keep], NN, preferred_element_type=F32)
+        mine = t_keep[...] + lax.dot_general(low, kmat[rows, keep], NN, preferred_element_type=F32)
         arrived(t_rc, R_TC)
         mine = mine + t_rc[...]
         for i in range(8):
@@ -214,10 +245,26 @@
     def phase_across():
         arrived(rs_t, R_RT)
         x_src[...] = eight(rs_t)
-        send(x_src, x_buf.at[(x - k + 3) % 4], S_X, R_X, device(k, y, z, c), off_diag)
+        send(x_src, x_buf.at[(x - k + 3) % 4], S_X, R_X, device(k, y, z, c), off_diag & later_pair)
+
+        @pl.when(first_pair)
+        def _():
+            first = len(pending)
+            spot = x_quad.at[x, 2 * h + c]
+            for n in (3, 2, 1):
+                send(x_src, spot, S_G + n, R_XQ, device(0, (h + n // 2) % 2, z, (c + n % 2) % 2))
+            send(x_src, spot, S_G, R_XQ, device(0, y, z, c), off_diag)
+            pl.when(diag)(lambda: stay(x_src, spot, R_XQ))
+            nested(first, first_pair)
 
     def phase_residual():
-        @pl.when(diag)
+        @pl.when(diag & first_pair)
+        def _():
+            arrived(x_quad, R_XQ)
+            for i in range(4):
+                inp[i] = (x_quad[0, i] + x_quad[1, i]) + (x_quad[2, i] + x_quad[3, i])
+
+        @pl.when(later_diag)
         def _():
             first = len(pending)
             arrived(x_buf, R_X)
@@ -231,13 +278,13 @@
                 send(s_src, inp.at[2 * h + c], S_G + n, R_IN,
                      device(x, 2 * k + (h + n // 2) % 2, z, (c + n % 2) % 2))
             stay(s_src, inp.at[2 * h + c], R_IN)
-            nested(first, diag)
+            nested(first, later_diag)
 
     def phase_product():
         @pl.when(works)
         def _():
             first = len(pending)
-            arrived(inp, R_IN)
+            pl.when(fed)(lambda: arrived(inp, R_IN))
             v = jnp.concatenate([inp[i] for i in range(4)], axis=1)
             high = v.astype(BF16)
             both = jnp.concatenate([high, (v - high.astype(F32)).astype(BF16)], axis=0)
@@ -290,6 +337,9 @@
             arrived(u_src, R_O1)
 
     def phase_results():
+        before = pending[:]
+        del pending[:]
+
         @pl.when(not_last)
         def _():
             first = len(pending)
@@ -300,11 +350,7 @@
                     send(u_src, o_buf.at[slot], S_O2 + 2 * n + e, R_O2, device(x, 2 * k + z // 4, zt, (c + e) % 2))
             send(u_src, o_buf.at[slot], S_O2 + 14, R_O2, device(x, 2 * k + z // 4, z, 1 - c))
             send(u_src, o_buf.at[slot], S_O2 + 15, R_O2, device(x, 2 * k + z // 4, z, c), out_away)
-
-            @pl.when(out_own)
-            def _():
-                stay(u_src, o_buf.at[slot], R_O2)
-            arrived(o_buf, R_O2)
+            pl.when(out_own)(lambda: stay(u_src, o_buf.at[slot], R_O2))
             nested(first, not_last)
 
         @pl.when(last)
@@ -314,20 +360,45 @@
             for n, d in enumerate(AROUND):
                 send(u_src, o_buf.at[slot], S_O2 + n, R_O2, device(x, y, (z + d) % 8, c))
             stay(u_src, o_buf.at[slot], R_O2)
+            nested(first, last)
+
+        for wait in before:
+            wait()
+
+        def write(start):
+            for i in range(8):
+                out_vm[:, pl.ds(pl.multiple_of((start + i) * 128, 128), 128)] = o_buf[start + i]
+            cols = pl.ds(pl.multiple_of(start * 128, 1024), 1024)
+            pltpu.make_async_copy(out_vm.at[:, cols], out.at[:, cols], rsem.at[L_O]).start()
+
+        @pl.when(not_last)
+        def _():
+            arrived(o_buf, R_O2)
+            write(0)
+            write(8)
+
+        @pl.when(last)
+        def _():
+            first = len(pending)
             mine = o_buf.at[pl.ds(c * 8, 8)]
             arrived(mine, R_O2)
             send(mine, mine, S_O3, R_O3, partner, None, lambda: o_buf.at[0:8])
+            write(c * 8)
+            nested(first, last)
+        for wait in pending[:-1]:
+            wait()
+
+        @pl.when(last)
+        def _():
             arrived(o_buf.at[pl.ds(8 - c * 8, 8)], R_O3)
-            nested(first, last)
-        for i in range(16):
-            out[:, i * 128:(i + 1) * 128] = o_buf[i]
-
-    phases = (phase_images, phase_factor, phase_rounded, phase_totals, phase_across, phase_split, phase_residual,
+            write(8 - c * 8)
+        pending[-1]()
+        arrived(out_vm, L_O)
+
+    phases = (phase_images, phase_rounded, phase_totals, phase_across, phase_split, phase_residual,
               phase_product, phase_solved, phase_results)
     for phase in phases:
         phase()
-    for wait in pending:
-        wait()
 
 
 def body(points, centres, vector, factor):
@@ -339,14 +410,15 @@
         sweep_kernel,
         out_shape=jax.ShapeDtypeStruct((32, 2048), F32),
         in_specs=[any_space] * 4,
-        out_specs=pl.BlockSpec(memory_space=pltpu.VMEM),
+        out_specs=any_space,
         scratch_shapes=[
             pltpu.VMEM((1024, 512), BF16), pltpu.VMEM((2048, 512), BF16), pltpu.VMEM((32, 2048), F32),
-            pltpu.VMEM((1, 2048), F32), pltpu.VMEM((1024, 2048), BF16),
+            pltpu.VMEM((32, 2048), BF16), pltpu.VMEM((1, 2048), F32), pltpu.VMEM((1024, 2048), BF16),
             pltpu.VMEM((512, 1024), F32), pltpu.VMEM((512, 1024), BF16), pltpu.VMEM((512, 1024), BF16),
-            piece(8), piece(8), piece(), piece(8), pltpu.VMEM((32, 1024), BF16),
+            pltpu.VMEM((2, 8, 16, 128), F32), pltpu.VMEM((2, 8, 16, 128), F32), pltpu.VMEM((2, 16, 128), F32),
+            pltpu.VMEM((2, 8, 16, 128), F32), pltpu.VMEM((32, 1024), BF16), pltpu.VMEM((32, 1024), F32),
             pltpu.VMEM((32, 1024), F32), pltpu.VMEM((32, 1024), F32), piece(8), piece(8), piece(), piece(3),
-            piece(), piece(4), piece(8), piece(4, 8), piece(), piece(16),
+            piece(), piece(4), piece(8), piece(4, 8), piece(), piece(16), piece(4, 4), pltpu.VMEM((32, 2048), F32),
             pltpu.SemaphoreType.DMA((S_END,)), pltpu.SemaphoreType.DMA((R_END,)),
         ],
         compiler_params=pltpu.CompilerParams(

time: 122 us -> 119 us (0.975)
  Pallas kernels: 120 us -> 117 us
    pallas_call x1, Pallas kernels: 120 us -> 117 us  [body(): pl.pallas_call(sweep_kernel, out_shape=jax.ShapeDtypeStruct((32, 2048), F...]
where the time goes in v3:
time: 119 us
  Pallas kernels  117 us (98%)
  local copies, waits for them, and re-layouts  1.67 us (1%)
    pallas_call x1, Pallas kernels, body(): pl.pallas_call(sweep_kernel, out_shape=jax.ShapeDtypeStruct((32, 2048), F...  117 us

profile of v3, /device:TPU:57, one launch (start us, length us, event | category | flops | bytes accessed | tf_op | source)
XLA Modules:
  0.0 118.7 jit_solution(15139060524294377074)
XLA Ops:
  0.0 117.1 %shard_map.46 = f32[32,2048]{1,0:T(8,128)} custom-call(bf16[1024,512]{1,0:T(8,128)(2,1)} %points.1, bf16[2048,512]{1,0:T(8,128)(2,1)} %centres.1, f32[32,2048]{1,0:T(8,128)} %vector.1, f32[256,2048]{1,0:T(8,128)} %factor.1), custom_call_target="tpu_custom_call" | custom-call | flops 2147483648 | bytes 6291456 | tf_op jit(solution)/shard_map/pallas_call | solution.py:409
  117.1 1.7 %copy.6 = f32[32,2048]{1,0:T(8,128)} copy(f32[32,2048]{1,0:T(8,128)} %shard_map.46) | data formatting | bytes 524288

commit v4 on v3

--- a/solution.py
+++ b/solution.py
@@ -288,33 +288,34 @@
             v = jnp.concatenate([inp[i] for i in range(4)], axis=1)
             high = v.astype(BF16)
             both = jnp.concatenate([high, (v - high.astype(F32)).astype(BF16)], axis=0)
-            far = jnp.where(plain, (z // 4 + 1) % 2, (z + 1) % 2) * 4
-            for own_half in range(2):
-                start = far + own_half * (4 - 2 * far)
-                cols = pl.ds(pl.multiple_of(start * 128, 512), 512)
+            for i in range(4):
+                far = (i < 2) + 0
+                along = (z // 4 + far) % 2 * 4 + (2 * i if far else (z // 2 + 1 - i % 2) % 2 * 2)
+                dealt_out = (z + far) % 2 * 4 + (h + 1 - i % 2) % 2 * 2
+                start = jnp.where(plain, along, dealt_out)
+                cols = pl.ds(pl.multiple_of(start * 128, 256), 256)
                 prod = lax.dot_general(both, fhigh[:, cols], NN, preferred_element_type=F32)
                 rest = lax.dot_general(high, flow[:, cols], NN, preferred_element_type=F32)
                 part = prod[0:32] + (prod[32:64] + rest)
-                for i in range(4):
-                    ab_src[start + i] = part[:, i * 128:(i + 1) * 128]
+                ab_src[start] = part[:, 0:128]
+                ab_src[start + 1] = part[:, 128:256]
 
                 @pl.when(plain)
                 def _():
                     inside = len(pending)
-                    for n in range(4):
-                        g = start + (z + 2 + n) % 4
-                        if own_half and n == 2:
+                    for n in range(2):
+                        g = along + (z + 1 + n) % 2
+                        if i == 3 and n == 1:
                             stay(ab_src.at[g], rs_ab.at[x, z], R_AB + x)
                         else:
-                            send(ab_src.at[g], rs_ab.at[x, z], S_RA + 4 * own_half + n, R_AB + x,
+                            send(ab_src.at[g], rs_ab.at[x, z], S_RA + 2 * i + n, R_AB + x,
                                  device(x, y, g, c), None, lambda: ab_src.at[0])
                     nested(inside, plain)
 
                 @pl.when(dealt)
                 def _():
                     inside = len(pending)
-                    bits = (3, 2, 1, 0) if own_half else (7, 6, 5, 4)
-                    scatter(ab_src, rs_ab.at[x, z], S_RA, R_AB + x, k, ab_own, ab_away, bits)
+                    scatter(ab_src, rs_ab.at[x, z], S_RA, R_AB + x, k, ab_own, ab_away, (7 - 2 * i, 6 - 2 * i))
                     nested(inside, dealt)
             nested(first, works)
 

time: 119 us -> 120 us (level)
  no operation moved by 1% of the time
where the time goes in v4:
time: 120 us; the launch traced here: 119 us
  Pallas kernels  118 us (98%)
  local copies, waits for them, and re-layouts  1.67 us (1%)
    pallas_call x1, Pallas kernels, body(): pl.pallas_call(sweep_kernel, out_shape=jax.ShapeDtypeStruct((32, 2048), F...  118 us

profile of v4, /device:TPU:57, one launch (start us, length us, event | category | flops | bytes accessed | tf_op | source)
XLA Modules:
  0.0 119.4 jit_solution(17060412446443513644)
XLA Ops:
  0.0 117.8 %shard_map.46 = f32[32,2048]{1,0:T(8,128)} custom-call(bf16[1024,512]{1,0:T(8,128)(2,1)} %points.1, bf16[2048,512]{1,0:T(8,128)(2,1)} %centres.1, f32[32,2048]{1,0:T(8,128)} %vector.1, f32[256,2048]{1,0:T(8,128)} %factor.1), custom_call_target="tpu_custom_call" | custom-call | flops 2147483648 | bytes 6291456 | tf_op jit(solution)/shard_map/pallas_call | solution.py:410
  117.8 1.7 %copy.6 = f32[32,2048]{1,0:T(8,128)} copy(f32[32,2048]{1,0:T(8,128)} %shard_map.46) | data formatting | bytes 524288
